TPU v7x, 512 devices: a whole 4x4x16 slice. The times are simulated.
512 devices in a mesh: dp: 16 (over z), expert: 32 (over y, x, core).
Axes of the slice: x: 4, y: 4, z: 16, core: 2. Of those that a mesh axis runs over, the one named last changes fastest.
Arguments:
- tokens: bfloat16 [65536, 1024], P(('dp', 'expert')), may hold values from -6 to 6
- grad_out: bfloat16 [65536, 1024], P(('dp', 'expert')), may hold values from -6 to 6
- expert_ids: int32 [65536, 2], P(('dp', 'expert')), may hold values from 0 to 31, all different within a row; in each aligned block of 128 rows (0 to 127, 128 to 255, ...) at most 16 rows name the same one
- route_probs: bfloat16 [65536, 2], P(('dp', 'expert')), may hold values from 0.19921875 to 1
- gate_up_weight: bfloat16 [1024, 32, 1536], P('dp', 'expert'), may hold values from -0.1875 to 0.1875
- down_weight: bfloat16 [32, 768, 1024], P('expert'), may hold values from -0.21875 to 0.21875
- gate_up_scale_index: int32 [8, 32, 2], P(None, 'expert'), may hold values from 0 to 15
- down_scale_index: int32 [32, 6], P('expert'), may hold values from 0 to 15
- scale_table: float32 [16], replicated, may hold values from 0.5 to 2
Outputs:
- token_grad: bfloat16 [65536, 1024], P(('dp', 'expert'))
- prob_grad: float32 [65536, 2], P(('dp', 'expert'))
- gate_up_grad: bfloat16 [1024, 32, 1536], P('dp', 'expert')
- down_grad: bfloat16 [32, 768, 1024], P('expert')
Inputs may be any that keep to these rules, and one draw needn't show every extreme that they name: `expert_ids`: each row names two different experts. The 128 rows of one device name one expert at most 16 times, and in every draw some device's rows name some expert exactly 16 times.
All inputs are finite; a program needn't handle non-finite values.
Results may differ from a plain program's by a relative error of at most 0.022.
Values may be sent and summed in bfloat16 or wider, within the bound.
No kernel may reach another device: no remote copies, remote signals or barrier semaphores. Data moves between devices by JAX's collectives and lax.ppermute only.
A program may use at most 64 MiB of HBM per device.

v0:
```python
import jax
import jax.numpy as jnp
from jax import lax
from jax.sharding import PartitionSpec as P

QBLOCK = 128


def lookup(level_index, level_table):
    onehot = (level_index[..., None] == jnp.arange(level_table.shape[0], dtype=jnp.int32)).astype(
        level_table.dtype
    )
    return jnp.sum(onehot * level_table, axis=-1)


def slot_tables(routes, experts, capacity):
    flat_routes = routes.reshape(-1)
    expert_hits = (flat_routes[:, None] == jnp.arange(experts, dtype=jnp.int32)[None, :]).astype(
        jnp.int32
    )
    place = jnp.arange(flat_routes.shape[0], dtype=jnp.int32)
    earlier = (place[None, :] < place[:, None]).astype(jnp.bfloat16)
    before = jnp.dot(
        earlier, expert_hits.astype(jnp.bfloat16), preferred_element_type=jnp.float32
    ).astype(jnp.int32)
    slot_rank = jnp.sum(before * expert_hits, axis=1)
    destination = flat_routes * capacity + slot_rank
    table_hits = destination[:, None] == jnp.arange(experts * capacity, dtype=jnp.int32)[None, :]
    return table_hits.astype(jnp.float32).reshape(routes.shape[0], 2, experts * capacity)


def body(
    tokens,
    grad_out,
    expert_ids,
    route_probs,
    gate_up_weight,
    down_weight,
    gate_up_scale_index,
    down_scale_index,
    scale_table,
):
    high = lax.Precision.HIGHEST
    f32 = jnp.float32
    groups = lax.axis_size("expert")
    tok_dev = tokens.shape[0]
    model_width = tokens.shape[1]
    per_device = down_weight.shape[0]
    hidden = down_weight.shape[1]
    experts = per_device * groups
    capacity = 4 * tok_dev // experts
    slots_all = experts * capacity
    slot_hits = slot_tables(expert_ids, experts, capacity)
    either = (slot_hits[:, 0] + slot_hits[:, 1]).astype(jnp.bfloat16)
    row_shape = (groups, per_device, capacity, model_width)
    send_tokens = (
        jnp.einsum("ts,td->sd", either, tokens, preferred_element_type=f32)
        .astype(jnp.bfloat16)
        .reshape(row_shape)
    )
    send_grads = (
        jnp.einsum("ts,td->sd", either, grad_out, preferred_element_type=f32)
        .astype(jnp.bfloat16)
        .reshape(row_shape)
    )
    send_probs = (
        jnp.einsum("tks,tk->s", slot_hits, route_probs.astype(f32), precision=high)
        .astype(jnp.bfloat16)
        .reshape(row_shape[:3])
    )
    recv_tokens, recv_grads, recv_probs = (
        lax.all_to_all(send_tokens, "expert", split_axis=0, concat_axis=0, tiled=True),
        lax.all_to_all(send_grads, "expert", split_axis=0, concat_axis=0, tiled=True),
        lax.all_to_all(send_probs, "expert", split_axis=0, concat_axis=0, tiled=True),
    )
    level_rows = jnp.repeat(lookup(gate_up_scale_index, scale_table), QBLOCK, axis=0)
    full_scale = jnp.repeat(level_rows, hidden, axis=2)
    down_scale = jnp.repeat(lookup(down_scale_index, scale_table), QBLOCK, axis=1)
    down_eff = (down_weight.astype(f32) * down_scale[:, :, None]).astype(jnp.bfloat16)
    gathered = lax.all_gather(gate_up_weight, "dp", axis=0, tiled=True)
    gate_up_eff = (gathered.astype(f32) * full_scale).astype(jnp.bfloat16)
    projected = jnp.einsum("sjcd,djf->sjcf", recv_tokens, gate_up_eff, preferred_element_type=f32)
    gate_part = projected[..., :hidden]
    up_part = projected[..., hidden:]
    sigmoid_gate = jax.nn.sigmoid(gate_part)
    activated = gate_part * sigmoid_gate
    hidden_rows = (activated * up_part).astype(jnp.bfloat16)
    hidden_grad = jnp.einsum("sjcd,jfd->sjcf", recv_grads, down_eff, preferred_element_type=f32)
    probs_wide = recv_probs.astype(f32)[..., None]
    scaled_grad = probs_wide * hidden_grad
    gate_grad = scaled_grad * up_part * sigmoid_gate * (1.0 + gate_part * (1.0 - sigmoid_gate))
    up_grad = scaled_grad * activated
    joint_grad = jnp.concatenate([gate_grad, up_grad], axis=-1).astype(jnp.bfloat16)
    row_grads = jnp.einsum(
        "sjcf,djf->sjcd", joint_grad, gate_up_eff, preferred_element_type=f32
    ).astype(jnp.bfloat16)
    back_rows = lax.all_to_all(row_grads, "expert", split_axis=0, concat_axis=0, tiled=True)
    token_grad = jnp.dot(
        either, back_rows.reshape(slots_all, model_width), preferred_element_type=f32
    ).astype(jnp.bfloat16)
    expert_out = jnp.einsum("sjcf,jfd->sjcd", hidden_rows, down_eff, preferred_element_type=f32)
    back_out = lax.all_to_all(
        expert_out.astype(jnp.bfloat16), "expert", split_axis=0, concat_axis=0, tiled=True
    ).astype(expert_out.dtype)
    picked = jnp.einsum(
        "tks,sd->tkd", slot_hits, back_out.reshape(slots_all, model_width), precision=high
    )
    prob_grad = jnp.sum(picked * grad_out.astype(f32)[:, None, :], axis=-1)
    weighted = (probs_wide * hidden_rows.astype(f32)).astype(jnp.bfloat16)
    partial_sum = jnp.einsum("sjcd,sjcf->djf", recv_tokens, joint_grad, preferred_element_type=f32)
    gate_up_grad = lax.psum_scatter(
        (partial_sum * full_scale).astype(jnp.bfloat16), "dp", scatter_dimension=0, tiled=True
    )
    down_part = (
        jnp.einsum("sjcf,sjcd->jfd", weighted, recv_grads, preferred_element_type=f32)
        * down_scale[:, :, None]
    )
    down_grad = lax.psum(down_part.astype(jnp.bfloat16), "dp")
    return (token_grad, prob_grad, gate_up_grad, down_grad)


def solution(mesh):
    in_specs = (
        P(("dp", "expert"), None),
        P(("dp", "expert"), None),
        P(("dp", "expert"), None),
        P(("dp", "expert"), None),
        P("dp", "expert", None),
        P("expert", None, None),
        P(None, "expert", None),
        P("expert", None),
        P(),
    )
    out_specs = (
        P(("dp", "expert"), None),
        P(("dp", "expert"), None),
        P("dp", "expert", None),
        P("expert", None, None),
    )
    return jax.shard_map(body, mesh=mesh, in_specs=in_specs, out_specs=out_specs, check_vma=False)
```

profile of v0, /device:TPU:2, one launch (start us, length us, event | category | flops | bytes accessed | tf_op | source)
XLA Modules:
  0.0 353.9 jit_solution(2334480392853353179)
XLA Ops:
  11.6 9.4 %all-to-all-start = ((bf16[32,1,16]{2,1,0:T(2,128)(2,1)}), bf16[32,1,16]{2,1,0:T(2,128)(2,1)S(1)}, u32[]{:S(2)}, u32[]{:S(2)}) async-start(bf16[32,1,16]{2,1,0:T(2,128)(2,1)} %reshape.246), calls=%async_computation | async-start | bytes 32768 | tf_op jit(solution)/shard_map/all_to_all | solution.py:74
  22.6 4.5 %all-to-all-done = bf16[32,1,16]{2,1,0:T(2,128)(2,1)S(1)} async-done(((bf16[32,1,16]{2,1,0:T(2,128)(2,1)}), bf16[32,1,16]{2,1,0:T(2,128)(2,1)S(1)}, u32[]{:S(2)}, u32[]{:S(2)}) %all-to-all-start) | async-done | bytes 1056 | tf_op jit(solution)/shard_map/all_to_all | solution.py:74
  27.2 5.7 %all-to-all-start.2 = ((bf16[32,1,16,1024]{3,2,1,0:T(8,128)(2,1)}), bf16[32,1,16,1024]{3,2,1,0:T(8,128)(2,1)}, u32[]{:S(2)}, u32[]{:S(2)}) async-start(bf16[32,1,16,1024]{3,2,1,0:T(8,128)(2,1)} %bitcast.19), calls=%async_computation.2 | async-start | bytes 2097152 | tf_op jit(solution)/shard_map/all_to_all | solution.py:72
  35.5 55.5 %all-gather.2.cloned.1.call-done = bf16[1024,1,1536]{2,0,1:T(8,128)(2,1)} async-done(((bf16[64,1,1536]{2,0,1:T(8,128)(2,1)}), bf16[1024,1,1536]{2,0,1:T(8,128)(2,1)}) %all-gather.2.cloned.1.call-update) | async-done | bytes 3145744 | tf_op jit(solution)/shard_map/all_gather | solution.py:80
  91.0 3.2 copy.76
  94.2 7.2 %all-to-all-start.1 = ((bf16[32,1,16,1024]{3,2,1,0:T(8,128)(2,1)}), bf16[32,1,16,1024]{3,2,1,0:T(8,128)(2,1)}, u32[]{:S(2)}, u32[]{:S(2)}) async-start(bf16[32,1,16,1024]{3,2,1,0:T(8,128)(2,1)} %bitcast.139), calls=%async_computation.1 | async-start | bytes 2097152 | tf_op jit(solution)/shard_map/all_to_all | solution.py:73
  103.7 1.7 copy-done.1
  105.4 1.7 copy-done.2
  107.1 5.1 %convolution_bitcast_fusion = f32[32,1,16,1536]{3,0,2,1:T(8,128)} fusion(bf16[1024,1536,1]{0,1,2:T(8,128)(2,1)S(1)} %fusion.3, bf16[32,1,16,1024]{3,2,1,0:T(8,128)(2,1)} %all-to-all-done.2), kind=kOutput, calls=%fused_computation.4 | convolution fusion | flops 1610612736 | bytes 7340032 | tf_op jit(solution)/shard_map/sjcd,djf->sjcf/dot_general | solution.py:82
  112.2 5.5 %all-to-all-done.1 = bf16[32,1,16,1024]{3,2,1,0:T(8,128)(2,1)} async-done(((bf16[32,1,16,1024]{3,2,1,0:T(8,128)(2,1)}), bf16[32,1,16,1024]{3,2,1,0:T(8,128)(2,1)}, u32[]{:S(2)}, u32[]{:S(2)}) %all-to-all-start.1) | async-done | bytes 1048608 | tf_op jit(solution)/shard_map/all_to_all | solution.py:73
  117.6 5.3 %fusion.31 = (bf16[32,16,768]{2,0,1:T(8,128)(2,1)S(1)}, bf16[32,16,768]{2,0,1:T(8,128)(2,1)S(1)}, bf16[32,1,16,768]{3,0,2,1:T(8,128)(2,1)}) fusion(f32[32,1,16,1536]{3,0,2,1:T(8,128)} %convolution_bitcast_fusion, bf16[32,1,16,1024]{3,2,1,0:T(8,128)(2,1)} %all-to-all-done.1, bf16[1,768,1024]{2,1,0:T(8,128)(2,1)S(1)} %copy-done.11, f32[768]{0:T(1024)S(1)} %copy-done.8, ...), kind=kOutput, calls=%fused_computation.49 | convolution fusion | flops 813957120 | bytes 8131584 | tf_op jit(solution)/shard_map/sjcd,jfd->sjcf/dot_general | solution.py:88
  123.0 3.8 %fusion.17 = f32[1536,1024,1]{1,0,2:T(8,128)S(1)} fusion(bf16[32,16,768]{2,0,1:T(8,128)(2,1)S(1)} %get-tuple-element.25, bf16[32,16,768]{2,0,1:T(8,128)(2,1)S(1)} %get-tuple-element.24, bf16[32,1,16,1024]{3,2,1,0:T(8,128)(2,1)} %all-to-all-done.2), kind=kOutput, calls=%fused_computation.36 | convolution fusion | flops 1613758464 | bytes 8912896 | tf_op jit(solution)/shard_map/sjcd,sjcf->djf/dot_general | solution.py:110
  126.8 1.8 fusion.2
  128.6 3.0 copy.96
  135.8 5.7 %all-to-all-start.4 = ((bf16[32,1,16,1024]{3,2,1,0:T(8,128)(2,1)}), bf16[32,1,16,1024]{3,2,1,0:T(8,128)(2,1)}, u32[]{:S(2)}, u32[]{:S(2)}) async-start(bf16[32,1,16,1024]{3,2,1,0:T(8,128)(2,1)} %copy.86), calls=%async_computation.4 | async-start | bytes 2097152 | tf_op jit(solution)/shard_map/all_to_all | solution.py:102
  141.8 4.1 %fusion.11 = bf16[1,768,1024]{2,1,0:T(8,128)(2,1)} fusion(f32[768]{0:T(1024)S(1)} %copy-done.8, bf16[32,1,16,1024]{3,2,1,0:T(8,128)(2,1)} %all-to-all-done.1, bf16[32,1,16,768]{3,0,2,1:T(8,128)(2,1)} %get-tuple-element.26, f32[32,16]{0,1:T(8,128)S(1)} %copy.78), kind=kOutput, calls=%fused_computation.23 | convolution fusion | flops 808058880 | bytes 3412992 | tf_op jit(solution)/shard_map/sjcf,sjcd->jfd/dot_general | solution.py:115
  146.0 3.2 fusion.13
  150.7 7.1 %all-to-all-done.4 = bf16[32,1,16,1024]{3,2,1,0:T(8,128)(2,1)} async-done(((bf16[32,1,16,1024]{3,2,1,0:T(8,128)(2,1)}), bf16[32,1,16,1024]{3,2,1,0:T(8,128)(2,1)}, u32[]{:S(2)}, u32[]{:S(2)}) %all-to-all-start.4) | async-done | bytes 1048608 | tf_op jit(solution)/shard_map/all_to_all | solution.py:102
  157.8 5.0 %all-to-all-start.3 = ((bf16[32,1,16,1024]{3,2,1,0:T(8,128)(2,1)}), bf16[32,1,16,1024]{3,2,1,0:T(8,128)(2,1)S(1)}, u32[]{:S(2)}, u32[]{:S(2)}) async-start(bf16[32,1,16,1024]{3,2,1,0:T(8,128)(2,1)} %copy.85), calls=%async_computation.3 | async-start | bytes 2097152 | tf_op jit(solution)/shard_map/all_to_all | solution.py:97
  162.9 2.4 fusion.14
  165.3 13.8 %all-to-all-done.3 = bf16[32,1,16,1024]{3,2,1,0:T(8,128)(2,1)S(1)} async-done(((bf16[32,1,16,1024]{3,2,1,0:T(8,128)(2,1)}), bf16[32,1,16,1024]{3,2,1,0:T(8,128)(2,1)S(1)}, u32[]{:S(2)}, u32[]{:S(2)}) %all-to-all-start.3) | async-done | bytes 1048608 | tf_op jit(solution)/shard_map/all_to_all | solution.py:97
  180.1 22.4 %reduce-scatter.4.cloned.1.call-done = bf16[64,1536]{1,0:T(8,128)(2,1)} async-done(((bf16[1024,1536]{1,0:T(8,128)(2,1)}), bf16[64,1536]{1,0:T(8,128)(2,1)}) %reduce-scatter.4.cloned.1.call-update) | async-done | bytes 196624
  204.5 140.2 %all-reduce.2.cloned.1.call-done = bf16[1,768,1024]{2,1,0:T(8,128)(2,1)} async-done(((bf16[1,768,1024]{2,1,0:T(8,128)(2,1)}), bf16[1,768,1024]{2,1,0:T(8,128)(2,1)}) %all-reduce.2.cloned.1.call-update) | async-done | bytes 1572880 | tf_op jit(solution)/shard_map/psum | solution.py:118
  344.7 2.7 copy.122
  (73 shorter events, 20.0 us)
Async XLA Ops:
  7.2 14.0 %copy-start = (bf16[128,1024]{1,0:T(8,128)(2,1)S(1)}, bf16[128,1024]{1,0:T(8,128)(2,1)}, u32[]{:S(2)}) copy-start(bf16[128,1024]{1,0:T(8,128)(2,1)} %param.9) | copy-start | bytes 786436
  7.2 83.9 %all-gather.2.cloned.1.call-start = ((), (), s32[]{:S(2)}) async-start(), calls=%async_computation.6 | async-start | bytes 3342336 | tf_op jit(solution)/shard_map/all_gather | solution.py:80
  10.0 11.0 %copy-start.6 = (s32[128,2]{0,1:T(2,128)}, s32[128,2]{0,1:T(2,128)S(1)}, u32[]{:S(2)}) copy-start(s32[128,2]{0,1:T(2,128)S(1)} %multiply_add_fusion) | copy-start | bytes 3076
  11.6 15.6 %all-to-all-start = ((bf16[32,1,16]{2,1,0:T(2,128)(2,1)}), bf16[32,1,16]{2,1,0:T(2,128)(2,1)S(1)}, u32[]{:S(2)}, u32[]{:S(2)}) async-start(bf16[32,1,16]{2,1,0:T(2,128)(2,1)} %reshape.246), calls=%async_computation | async-start | bytes 32768 | tf_op jit(solution)/shard_map/all_to_all | solution.py:74
  21.1 11.8 %copy-start.9 = (s32[8,1,2]{0,2,1:T(2,128)S(1)}, s32[8,1,2]{0,2,1:T(2,128)}, u32[]{:S(2)}) copy-start(s32[8,1,2]{0,2,1:T(2,128)} %param.15) | copy-start | bytes 196
  21.1 11.8 %copy-start.10 = (f32[16]{0:T(128)S(1)}, f32[16]{0:T(128)}, u32[]{:S(2)}) copy-start(f32[16]{0:T(128)} %param.17) | copy-start | bytes 196
  21.1 12.0 %copy-start.13 = (s32[1,6]{1,0:T(1,128)S(1)}, s32[1,6]{1,0:T(1,128)}, u32[]{:S(2)}) copy-start(s32[1,6]{1,0:T(1,128)} %param.16) | copy-start | bytes 76
  21.2 12.9 %copy-start.4 = (bf16[128,1024]{1,0:T(8,128)(2,1)S(1)}, bf16[128,1024]{1,0:T(8,128)(2,1)}, u32[]{:S(2)}) copy-start(bf16[128,1024]{1,0:T(8,128)(2,1)} %param.10) | copy-start | bytes 786436
  27.2 67.1 %all-to-all-start.2 = ((bf16[32,1,16,1024]{3,2,1,0:T(8,128)(2,1)}), bf16[32,1,16,1024]{3,2,1,0:T(8,128)(2,1)}, u32[]{:S(2)}, u32[]{:S(2)}) async-start(bf16[32,1,16,1024]{3,2,1,0:T(8,128)(2,1)} %bitcast.19), calls=%async_computation.2 | async-start | bytes 2097152 | tf_op jit(solution)/shard_map/all_to_all | solution.py:72
  94.2 23.4 %all-to-all-start.1 = ((bf16[32,1,16,1024]{3,2,1,0:T(8,128)(2,1)}), bf16[32,1,16,1024]{3,2,1,0:T(8,128)(2,1)}, u32[]{:S(2)}, u32[]{:S(2)}) async-start(bf16[32,1,16,1024]{3,2,1,0:T(8,128)(2,1)} %bitcast.139), calls=%async_computation.1 | async-start | bytes 2097152 | tf_op jit(solution)/shard_map/all_to_all | solution.py:73
  101.5 101.0 %reduce-scatter.4.cloned.1.call-start = ((), (), s32[]{:S(2)}) async-start(), calls=%async_computation.8 | async-start | bytes 3342336
  102.5 2.9 copy-start.1
  107.1 10.6 %copy-start.8 = (f32[768]{0:T(1024)S(1)}, f32[768]{0:T(1024)}, u32[]{:S(2)}) copy-start(f32[768]{0:T(1024)} %broadcast_bitcast_fusion.1) | copy-start | bytes 9220
  107.1 10.6 %copy-start.11 = (bf16[1,768,1024]{2,1,0:T(8,128)(2,1)S(1)}, bf16[1,768,1024]{2,1,0:T(8,128)(2,1)}, u32[]{:S(2)}) copy-start(bf16[1,768,1024]{2,1,0:T(8,128)(2,1)} %param.14) | copy-start | bytes 4718596
  117.6 9.2 %slice-start = ((s8[6291456]{0:T(1024)(128)(4,1)}), s8[4194304]{0:T(1024)(128)(4,1)S(1)}, s32[]{:S(2)}) async-start(s8[6291456]{0:T(1024)(128)(4,1)} %bitcast.136), calls=%async_computation.9 | async-start | bytes 8388608
  122.9 3.8 %copy-start.15 = (bf16[32,16,768]{2,0,1:T(8,128)(2,1)}, bf16[32,16,768]{2,0,1:T(8,128)(2,1)S(1)}, u32[]{:S(2)}) copy-start(bf16[32,16,768]{2,0,1:T(8,128)(2,1)S(1)} %get-tuple-element.24) | copy-start | bytes 2359300
  122.9 3.8 %copy-start.16 = (bf16[32,16,768]{2,0,1:T(8,128)(2,1)}, bf16[32,16,768]{2,0,1:T(8,128)(2,1)S(1)}, u32[]{:S(2)}) copy-start(bf16[32,16,768]{2,0,1:T(8,128)(2,1)S(1)} %get-tuple-element.25) | copy-start | bytes 2359300
  123.0 3.9 %slice-start.1 = ((s8[6291456]{0:T(1024)(128)(4,1)}), s8[2097152]{0:T(1024)(128)(4,1)S(1)}, s32[]{:S(2)}) async-start(s8[6291456]{0:T(1024)(128)(4,1)} %bitcast.136), calls=%async_computation.10 | async-start | bytes 4194304
  135.8 22.0 %all-to-all-start.4 = ((bf16[32,1,16,1024]{3,2,1,0:T(8,128)(2,1)}), bf16[32,1,16,1024]{3,2,1,0:T(8,128)(2,1)}, u32[]{:S(2)}, u32[]{:S(2)}) async-start(bf16[32,1,16,1024]{3,2,1,0:T(8,128)(2,1)} %copy.86), calls=%async_computation.4 | async-start | bytes 2097152 | tf_op jit(solution)/shard_map/all_to_all | solution.py:102
  141.6 4.4 %copy-start.3 = (bf16[1024,1536,1]{0,1,2:T(8,128)(2,1)S(1)}, bf16[1024,1536,1]{0,1,2:T(8,128)(2,1)}, u32[]{:S(2)}) copy-start(bf16[1024,1536,1]{0,1,2:T(8,128)(2,1)} %copy-done.2) | copy-start | bytes 9437188
  141.6 203.2 %all-reduce.2.cloned.1.call-start = ((), (), s32[]{:S(2)}) async-start(), calls=%async_computation.7 | async-start | bytes 3145728 | tf_op jit(solution)/shard_map/psum | solution.py:118
  149.1 13.7 %copy-start.5 = (bf16[128,1024]{1,0:T(8,128)(2,1)S(1)}, bf16[128,1024]{1,0:T(8,128)(2,1)}, u32[]{:S(2)}) copy-start(bf16[128,1024]{1,0:T(8,128)(2,1)} %param.10) | copy-start | bytes 786436
  149.1 13.8 %copy-start.7 = (s32[128,2]{0,1:T(2,128)S(1)}, s32[128,2]{0,1:T(2,128)}, u32[]{:S(2)}) copy-start(s32[128,2]{0,1:T(2,128)} %copy-done.6) | copy-start | bytes 3076
  157.8 21.3 %all-to-all-start.3 = ((bf16[32,1,16,1024]{3,2,1,0:T(8,128)(2,1)}), bf16[32,1,16,1024]{3,2,1,0:T(8,128)(2,1)S(1)}, u32[]{:S(2)}, u32[]{:S(2)}) async-start(bf16[32,1,16,1024]{3,2,1,0:T(8,128)(2,1)} %copy.85), calls=%async_computation.3 | async-start | bytes 2097152 | tf_op jit(solution)/shard_map/all_to_all | solution.py:97
  (3 other events, 4.7 us)
Sparse Core Ops, SparseCore 0:
  10.1 80.9 all-gather.1
  131.7 70.7 reduce-scatter.3
  205.4 139.2 all-reduce.1
where the time goes:
time: 355 us; the launch traced here: 354 us
  waiting for transfers between devices  250 us (70%)
  starting transfers between devices  33.6 us (9%)
  matrix products  29.9 us (8%)
  local copies, waits for them, and re-layouts  22.4 us (6%)
  between operations  14.1 us (4%)
  other arithmetic  4.22 us (1%)
    psum x1, waiting for transfers between devices, body(): down_grad = lax.psum(down_part.astype(jnp.bfloat16), 'dp')  140 us
    all_gather x1, waiting for transfers between devices, body(): gathered = lax.all_gather(gate_up_weight, 'dp', axis=0, tiled=True)  55.5 us
    unnamed x4, waiting for transfers between devices  23.1 us
    all_to_all x1, waiting for transfers between devices, body(): lax.all_to_all(row_grads, 'expert', split_axis=0, concat_axis=0, tiled=True)  13.8 us
    unnamed x45, local copies, waits for them, and re-layouts  13.5 us
    all_to_all x1, starting transfers between devices, body(): lax.all_to_all(send_probs, 'expert', split_axis=0, concat_axis=0, tiled=T...  9.4 us
    all_to_all x1, starting transfers between devices, body(): lax.all_to_all(send_grads, 'expert', split_axis=0, concat_axis=0, tiled=T...  7.21 us
    all_to_all x1, waiting for transfers between devices, body(): lax.all_to_all(expert_out.astype(jnp.bfloat16), 'expert', split_axis=0, c...  7.1 us
  transfers between devices with their start and end apart: 8, of which 7 were waited for; matrix products, arithmetic and copies ran while one was open for 10% of the time, Pallas kernels for 0%

commit v1 on v0

--- a/solution.py
+++ b/solution.py
@@ -77,7 +77,12 @@
     full_scale = jnp.repeat(level_rows, hidden, axis=2)
     down_scale = jnp.repeat(lookup(down_scale_index, scale_table), QBLOCK, axis=1)
     down_eff = (down_weight.astype(f32) * down_scale[:, :, None]).astype(jnp.bfloat16)
-    gathered = lax.all_gather(gate_up_weight, "dp", axis=0, tiled=True)
+    ring = [gate_up_weight]
+    for hop in range(15):
+        ring.append(lax.ppermute(ring[-1], "dp", [(dev, (dev + 1) % 16) for dev in range(16)]))
+    gathered = jnp.roll(
+        jnp.concatenate(ring[::-1], axis=0), (lax.axis_index("dp") + 1) * ring[0].shape[0], axis=0
+    )
     gate_up_eff = (gathered.astype(f32) * full_scale).astype(jnp.bfloat16)
     projected = jnp.einsum("sjcd,djf->sjcf", recv_tokens, gate_up_eff, preferred_element_type=f32)
     gate_part = projected[..., :hidden]

time: 355 us -> 484 us (1.36)
  waiting for transfers between devices: 250 us -> 322 us
  starting transfers between devices: 33.6 us -> 64.4 us
  local copies, waits for them, and re-layouts: 22.4 us -> 41.3 us
    ppermute x0 -> x15, waiting for transfers between devices: none -> 136 us  [body(): lax.ppermute(ring[-1], 'dp', [(dev, (dev + 1) % 16) for dev in range(16)])]
    all_gather x1 -> x0, waiting for transfers between devices: 55.5 us -> none  [body(): gathered = lax.all_gather(gate_up_weight, 'dp', axis=0, tiled=True)]
    ppermute x0 -> x15, starting transfers between devices: none -> 30.6 us  [body(): lax.ppermute(ring[-1], 'dp', [(dev, (dev + 1) % 16) for dev in range(16)])]
    concatenate x0 -> x1, local copies, waits for them, and re-layouts: none -> 15.8 us  [body(): jnp.roll(jnp.concatenate(ring[::-1], axis=0), (lax.axis_index('dp') + 1)...]
    unnamed x45 -> x44, local copies, waits for them, and re-layouts: 13.5 us -> 19 us
    unnamed x4 -> x3, waiting for transfers between devices: 23.1 us -> 23 us
  transfers between devices with their start and end apart: 8 -> 22, of which waited for: 7 -> 19; matrix products, arithmetic and copies ran while one was open for 10% -> 12% of each run, Pallas kernels for 0% -> 0%
where the time goes in v1:
time: 484 us; the launch traced here: 481 us
  waiting for transfers between devices  322 us (67%)
  starting transfers between devices  64.4 us (13%)
  local copies, waits for them, and re-layouts  41.3 us (9%)
  matrix products  32.1 us (7%)
  between operations  14.5 us (3%)
  other arithmetic  7.1 us (1%)
    psum x1, waiting for transfers between devices, body(): down_grad = lax.psum(down_part.astype(jnp.bfloat16), 'dp')  140 us
    ppermute x15, waiting for transfers between devices, body(): lax.ppermute(ring[-1], 'dp', [(dev, (dev + 1) % 16) for dev in range(16)])  136 us
    ppermute x15, starting transfers between devices, body(): lax.ppermute(ring[-1], 'dp', [(dev, (dev + 1) % 16) for dev in range(16)])  30.6 us
    unnamed x3, waiting for transfers between devices  23 us
    unnamed x44, local copies, waits for them, and re-layouts  19 us
    concatenate x1, local copies, waits for them, and re-layouts, body(): jnp.roll(jnp.concatenate(ring[::-1], axis=0), (lax.axis_index('dp') + 1)...  15.8 us
    all_to_all x1, waiting for transfers between devices, body(): lax.all_to_all(row_grads, 'expert', split_axis=0, concat_axis=0, tiled=True)  13.8 us
  transfers between devices with their start and end apart: 22, of which 19 were waited for; matrix products, arithmetic and copies ran while one was open for 12% of the time, Pallas kernels for 0%

profile of v1, /device:TPU:2, one launch (start us, length us, event | category | flops | bytes accessed | tf_op | source)
XLA Modules:
  0.0 481.3 jit_solution(1390742933998654442)
XLA Ops:
  12.2 16.7 %collective-permute-done = bf16[64,1,1536]{0,2,1:T(8,128)(2,1)S(1)} collective-permute-done((bf16[64,1,1536]{0,2,1:T(8,128)(2,1)S(1)}, bf16[64,1,1536]{0,2,1:T(8,128)(2,1)S(1)}, u32[]{:S(2)}, u32[]{:S(2)}) %collective-permute-start) | collective-permute-done | bytes 196640 | tf_op jit(solution)/shard_map/ppermute | solution.py:82
  30.8 11.5 %collective-permute-done.1 = bf16[64,1,1536]{0,2,1:T(8,128)(2,1)S(1)} collective-permute-done((bf16[64,1,1536]{0,2,1:T(8,128)(2,1)S(1)}, bf16[64,1,1536]{0,2,1:T(8,128)(2,1)S(1)}, u32[]{:S(2)}, u32[]{:S(2)}) %collective-permute-start.1) | collective-permute-done | bytes 196640 | tf_op jit(solution)/shard_map/ppermute | solution.py:82
  44.2 10.6 %collective-permute-done.2 = bf16[64,1,1536]{0,2,1:T(8,128)(2,1)S(1)} collective-permute-done((bf16[64,1,1536]{0,2,1:T(8,128)(2,1)S(1)}, bf16[64,1,1536]{0,2,1:T(8,128)(2,1)S(1)}, u32[]{:S(2)}, u32[]{:S(2)}) %collective-permute-start.2) | collective-permute-done | bytes 196640 | tf_op jit(solution)/shard_map/ppermute | solution.py:82
  56.7 9.6 %collective-permute-done.3 = bf16[64,1,1536]{0,2,1:T(8,128)(2,1)S(1)} collective-permute-done((bf16[64,1,1536]{0,2,1:T(8,128)(2,1)S(1)}, bf16[64,1,1536]{0,2,1:T(8,128)(2,1)S(1)}, u32[]{:S(2)}, u32[]{:S(2)}) %collective-permute-start.3) | collective-permute-done | bytes 196640 | tf_op jit(solution)/shard_map/ppermute | solution.py:82
  68.2 9.0 %collective-permute-done.4 = bf16[64,1,1536]{0,2,1:T(8,128)(2,1)S(1)} collective-permute-done((bf16[64,1,1536]{0,2,1:T(8,128)(2,1)S(1)}, bf16[64,1,1536]{0,2,1:T(8,128)(2,1)S(1)}, u32[]{:S(2)}, u32[]{:S(2)}) %collective-permute-start.4) | collective-permute-done | bytes 196640 | tf_op jit(solution)/shard_map/ppermute | solution.py:82
  79.1 9.0 %collective-permute-done.5 = bf16[64,1,1536]{0,2,1:T(8,128)(2,1)S(1)} collective-permute-done((bf16[64,1,1536]{0,2,1:T(8,128)(2,1)S(1)}, bf16[64,1,1536]{0,2,1:T(8,128)(2,1)S(1)}, u32[]{:S(2)}, u32[]{:S(2)}) %collective-permute-start.5) | collective-permute-done | bytes 196640 | tf_op jit(solution)/shard_map/ppermute | solution.py:82
  91.3 8.7 %collective-permute-done.6 = bf16[64,1,1536]{0,2,1:T(8,128)(2,1)S(1)} collective-permute-done((bf16[64,1,1536]{0,2,1:T(8,128)(2,1)S(1)}, bf16[64,1,1536]{0,2,1:T(8,128)(2,1)S(1)}, u32[]{:S(2)}, u32[]{:S(2)}) %collective-permute-start.6) | collective-permute-done | bytes 196640 | tf_op jit(solution)/shard_map/ppermute | solution.py:82
  102.7 10.2 %collective-permute-done.7 = bf16[64,1,1536]{0,2,1:T(8,128)(2,1)} collective-permute-done((bf16[64,1,1536]{0,2,1:T(8,128)(2,1)S(1)}, bf16[64,1,1536]{0,2,1:T(8,128)(2,1)}, u32[]{:S(2)}, u32[]{:S(2)}) %collective-permute-start.7) | collective-permute-done | bytes 196640 | tf_op jit(solution)/shard_map/ppermute | solution.py:82
  116.4 7.6 %all-to-all-start = ((bf16[32,1,16]{2,1,0:T(2,128)(2,1)}), bf16[32,1,16]{2,1,0:T(2,128)(2,1)S(1)}, u32[]{:S(2)}, u32[]{:S(2)}) async-start(bf16[32,1,16]{2,1,0:T(2,128)(2,1)} %reshape.246), calls=%async_computation | async-start | bytes 32768 | tf_op jit(solution)/shard_map/all_to_all | solution.py:74
  126.1 12.7 %collective-permute-done.9 = bf16[64,1,1536]{0,2,1:T(8,128)(2,1)S(1)} collective-permute-done((bf16[64,1,1536]{0,2,1:T(8,128)(2,1)}, bf16[64,1,1536]{0,2,1:T(8,128)(2,1)S(1)}, u32[]{:S(2)}, u32[]{:S(2)}) %collective-permute-start.9) | collective-permute-done | bytes 196640 | tf_op jit(solution)/shard_map/ppermute | solution.py:82
  140.8 11.9 %collective-permute-done.10 = bf16[64,1,1536]{0,2,1:T(8,128)(2,1)} collective-permute-done((bf16[64,1,1536]{0,2,1:T(8,128)(2,1)S(1)}, bf16[64,1,1536]{0,2,1:T(8,128)(2,1)}, u32[]{:S(2)}, u32[]{:S(2)}) %collective-permute-start.10) | collective-permute-done | bytes 196640 | tf_op jit(solution)/shard_map/ppermute | solution.py:82
  156.1 7.2 %all-to-all-start.2 = ((bf16[32,1,16,1024]{3,2,1,0:T(8,128)(2,1)}), bf16[32,1,16,1024]{3,2,1,0:T(8,128)(2,1)}, u32[]{:S(2)}, u32[]{:S(2)}) async-start(bf16[32,1,16,1024]{3,2,1,0:T(8,128)(2,1)} %bitcast.19), calls=%async_computation.2 | async-start | bytes 2097152 | tf_op jit(solution)/shard_map/all_to_all | solution.py:72
  170.6 8.3 %collective-permute-done.12 = bf16[64,1,1536]{0,2,1:T(8,128)(2,1)} collective-permute-done((bf16[64,1,1536]{0,2,1:T(8,128)(2,1)}, bf16[64,1,1536]{0,2,1:T(8,128)(2,1)}, u32[]{:S(2)}, u32[]{:S(2)}) %collective-permute-start.12) | collective-permute-done | bytes 196640 | tf_op jit(solution)/shard_map/ppermute | solution.py:82
  183.3 8.2 %collective-permute-done.13 = bf16[64,1,1536]{0,2,1:T(8,128)(2,1)} collective-permute-done((bf16[64,1,1536]{0,2,1:T(8,128)(2,1)}, bf16[64,1,1536]{0,2,1:T(8,128)(2,1)}, u32[]{:S(2)}, u32[]{:S(2)}) %collective-permute-start.13) | collective-permute-done | bytes 196640 | tf_op jit(solution)/shard_map/ppermute | solution.py:82
  195.5 7.6 %collective-permute-done.14 = bf16[64,1,1536]{0,2,1:T(8,128)(2,1)} collective-permute-done((bf16[64,1,1536]{0,2,1:T(8,128)(2,1)}, bf16[64,1,1536]{0,2,1:T(8,128)(2,1)}, u32[]{:S(2)}, u32[]{:S(2)}) %collective-permute-start.14) | collective-permute-done | bytes 196640 | tf_op jit(solution)/shard_map/ppermute | solution.py:82
  203.1 15.8 %concatenate.18 = bf16[2048,1,1536]{0,2,1:T(8,128)(2,1)} concatenate(bf16[64,1,1536]{0,2,1:T(8,128)(2,1)} %collective-permute-done.14, bf16[64,1,1536]{0,2,1:T(8,128)(2,1)} %collective-permute-done.13, bf16[64,1,1536]{0,2,1:T(8,128)(2,1)} %collective-permute-done.12, bf16[64,1,1536]{0,2,1:T(8,128)(2,1)} %collective-permute-done.11, bf16[64,1,1536]{0,2,1:T(8,128)(2,1)} %collective-permute-done.10, ...), dimensions={0} | concatenate | bytes 12582912 | tf_op jit(solution)/shard_map/jit(_roll_dynamic)/concatenate | solution.py:83
  219.0 7.8 %all-to-all-start.1 = ((bf16[32,1,16,1024]{3,2,1,0:T(8,128)(2,1)}), bf16[32,1,16,1024]{3,2,1,0:T(8,128)(2,1)S(1)}, u32[]{:S(2)}, u32[]{:S(2)}) async-start(bf16[32,1,16,1024]{3,2,1,0:T(8,128)(2,1)} %bitcast.13), calls=%async_computation.1 | async-start | bytes 2097152 | tf_op jit(solution)/shard_map/all_to_all | solution.py:73
  235.9 5.3 %convolution_bitcast_fusion = f32[32,1,16,1536]{3,0,2,1:T(8,128)} fusion(bf16[1024,1536,1]{0,1,2:T(8,128)(2,1)S(1)} %fusion.3, bf16[32,1,16,1024]{3,2,1,0:T(8,128)(2,1)} %all-to-all-done.2), kind=kOutput, calls=%fused_computation.4 | convolution fusion | flops 1610612736 | bytes 7340032 | tf_op jit(solution)/shard_map/sjcd,djf->sjcf/dot_general | solution.py:87
  242.9 5.3 %fusion.31 = (bf16[32,16,768]{2,0,1:T(8,128)(2,1)S(1)}, bf16[32,16,768]{2,0,1:T(8,128)(2,1)S(1)}, bf16[32,1,16,768]{3,0,2,1:T(8,128)(2,1)}) fusion(f32[32,1,16,1536]{3,0,2,1:T(8,128)} %convolution_bitcast_fusion, bf16[32,1,16,1024]{3,2,1,0:T(8,128)(2,1)S(1)} %all-to-all-done.1, bf16[1,768,1024]{2,1,0:T(8,128)(2,1)S(1)} %copy-done.12, ...), kind=kOutput, calls=%fused_computation.49 | convolution fusion | flops 813957120 | bytes 8131584 | tf_op jit(solution)/shard_map/sjcd,jfd->sjcf/dot_general | solution.py:93
  262.0 5.8 %all-to-all-start.4 = ((bf16[32,1,16,1024]{3,2,1,0:T(8,128)(2,1)}), bf16[32,1,16,1024]{3,2,1,0:T(8,128)(2,1)}, u32[]{:S(2)}, u32[]{:S(2)}) async-start(bf16[32,1,16,1024]{3,2,1,0:T(8,128)(2,1)} %copy.96), calls=%async_computation.4 | async-start | bytes 2097152 | tf_op jit(solution)/shard_map/all_to_all | solution.py:107
  276.9 7.1 %all-to-all-done.4 = bf16[32,1,16,1024]{3,2,1,0:T(8,128)(2,1)} async-done(((bf16[32,1,16,1024]{3,2,1,0:T(8,128)(2,1)}), bf16[32,1,16,1024]{3,2,1,0:T(8,128)(2,1)}, u32[]{:S(2)}, u32[]{:S(2)}) %all-to-all-start.4) | async-done | bytes 1048608 | tf_op jit(solution)/shard_map/all_to_all | solution.py:107
  291.5 13.8 %all-to-all-done.3 = bf16[32,1,16,1024]{3,2,1,0:T(8,128)(2,1)S(1)} async-done(((bf16[32,1,16,1024]{3,2,1,0:T(8,128)(2,1)}), bf16[32,1,16,1024]{3,2,1,0:T(8,128)(2,1)S(1)}, u32[]{:S(2)}, u32[]{:S(2)}) %all-to-all-start.3) | async-done | bytes 1048608 | tf_op jit(solution)/shard_map/all_to_all | solution.py:102
  306.3 23.0 %reduce-scatter.4.cloned.1.call-done = bf16[64,1536]{1,0:T(8,128)(2,1)} async-done(((bf16[1024,1536]{1,0:T(8,128)(2,1)}), bf16[64,1536]{1,0:T(8,128)(2,1)}) %reduce-scatter.4.cloned.1.call-update) | async-done | bytes 196624
  331.3 140.5 %all-reduce.2.cloned.1.call-done = bf16[1,768,1024]{2,1,0:T(8,128)(2,1)} async-done(((bf16[1,768,1024]{2,1,0:T(8,128)(2,1)}), bf16[1,768,1024]{2,1,0:T(8,128)(2,1)}) %all-reduce.2.cloned.1.call-update) | async-done | bytes 1572880 | tf_op jit(solution)/shard_map/psum | solution.py:123
  (99 shorter events, 93.6 us)
Async XLA Ops:
  7.2 147.5 %copy-start = (bf16[128,1024]{1,0:T(8,128)(2,1)S(1)}, bf16[128,1024]{1,0:T(8,128)(2,1)}, u32[]{:S(2)}) copy-start(bf16[128,1024]{1,0:T(8,128)(2,1)} %param.9) | copy-start | bytes 786436
  8.4 20.5 %collective-permute-start = (bf16[64,1,1536]{0,2,1:T(8,128)(2,1)S(1)}, bf16[64,1,1536]{0,2,1:T(8,128)(2,1)S(1)}, u32[]{:S(2)}, u32[]{:S(2)}) collective-permute-start(bf16[64,1,1536]{0,2,1:T(8,128)(2,1)S(1)} %copy.84), channel_id=1, source_target_pairs={{0,32},{32,64},{64,96},{96,128},{128,160},{160,192},{192,224},{224... | collective-permute-start | bytes 589832 | tf_op jit(solution)/shard_map/ppermute | solution.py:82
  28.9 13.4 %collective-permute-start.1 = (bf16[64,1,1536]{0,2,1:T(8,128)(2,1)S(1)}, bf16[64,1,1536]{0,2,1:T(8,128)(2,1)S(1)}, u32[]{:S(2)}, u32[]{:S(2)}) collective-permute-start(bf16[64,1,1536]{0,2,1:T(8,128)(2,1)S(1)} %collective-permute-done), channel_id=1, source_target_pairs={{0,32},{32,64},{64,96},{96,128},{128,160},{160,192},{192,224},{224... | collective-permute-start | bytes 589832 | tf_op jit(solution)/shard_map/ppermute | solution.py:82
  42.3 12.5 %collective-permute-start.2 = (bf16[64,1,1536]{0,2,1:T(8,128)(2,1)S(1)}, bf16[64,1,1536]{0,2,1:T(8,128)(2,1)S(1)}, u32[]{:S(2)}, u32[]{:S(2)}) collective-permute-start(bf16[64,1,1536]{0,2,1:T(8,128)(2,1)S(1)} %collective-permute-done.1), channel_id=1, source_target_pairs={{0,32},{32,64},{64,96},{96,128},{128,160},{160,192},{192,224},{224... | collective-permute-start | bytes 589832 | tf_op jit(solution)/shard_map/ppermute | solution.py:82
  54.8 11.6 %collective-permute-start.3 = (bf16[64,1,1536]{0,2,1:T(8,128)(2,1)S(1)}, bf16[64,1,1536]{0,2,1:T(8,128)(2,1)S(1)}, u32[]{:S(2)}, u32[]{:S(2)}) collective-permute-start(bf16[64,1,1536]{0,2,1:T(8,128)(2,1)S(1)} %collective-permute-done.2), channel_id=1, source_target_pairs={{0,32},{32,64},{64,96},{96,128},{128,160},{160,192},{192,224},{224... | collective-permute-start | bytes 589832 | tf_op jit(solution)/shard_map/ppermute | solution.py:82
  66.3 10.9 %collective-permute-start.4 = (bf16[64,1,1536]{0,2,1:T(8,128)(2,1)S(1)}, bf16[64,1,1536]{0,2,1:T(8,128)(2,1)S(1)}, u32[]{:S(2)}, u32[]{:S(2)}) collective-permute-start(bf16[64,1,1536]{0,2,1:T(8,128)(2,1)S(1)} %collective-permute-done.3), channel_id=1, source_target_pairs={{0,32},{32,64},{64,96},{96,128},{128,160},{160,192},{192,224},{224... | collective-permute-start | bytes 589832 | tf_op jit(solution)/shard_map/ppermute | solution.py:82
  77.2 10.9 %collective-permute-start.5 = (bf16[64,1,1536]{0,2,1:T(8,128)(2,1)S(1)}, bf16[64,1,1536]{0,2,1:T(8,128)(2,1)S(1)}, u32[]{:S(2)}, u32[]{:S(2)}) collective-permute-start(bf16[64,1,1536]{0,2,1:T(8,128)(2,1)S(1)} %collective-permute-done.4), channel_id=1, source_target_pairs={{0,32},{32,64},{64,96},{96,128},{128,160},{160,192},{192,224},{224... | collective-permute-start | bytes 589832 | tf_op jit(solution)/shard_map/ppermute | solution.py:82
  88.1 12.0 %collective-permute-start.6 = (bf16[64,1,1536]{0,2,1:T(8,128)(2,1)S(1)}, bf16[64,1,1536]{0,2,1:T(8,128)(2,1)S(1)}, u32[]{:S(2)}, u32[]{:S(2)}) collective-permute-start(bf16[64,1,1536]{0,2,1:T(8,128)(2,1)S(1)} %collective-permute-done.5), channel_id=1, source_target_pairs={{0,32},{32,64},{64,96},{96,128},{128,160},{160,192},{192,224},{224... | collective-permute-start | bytes 589832 | tf_op jit(solution)/shard_map/ppermute | solution.py:82
  100.0 12.8 %collective-permute-start.7 = (bf16[64,1,1536]{0,2,1:T(8,128)(2,1)S(1)}, bf16[64,1,1536]{0,2,1:T(8,128)(2,1)}, u32[]{:S(2)}, u32[]{:S(2)}) collective-permute-start(bf16[64,1,1536]{0,2,1:T(8,128)(2,1)S(1)} %collective-permute-done.6), channel_id=1, source_target_pairs={{0,32},{32,64},{64,96},{96,128},{128,160},{160,192},{192,224},{224... | collective-permute-start | bytes 589832 | tf_op jit(solution)/shard_map/ppermute | solution.py:82
  102.7 36.2 %copy-start.9 = (s32[128,2]{0,1:T(2,128)}, s32[128,2]{0,1:T(2,128)S(1)}, u32[]{:S(2)}) copy-start(s32[128,2]{0,1:T(2,128)S(1)} %multiply_add_fusion) | copy-start | bytes 3076
  112.9 11.2 %collective-permute-start.8 = (bf16[64,1,1536]{0,2,1:T(8,128)(2,1)}, bf16[64,1,1536]{0,2,1:T(8,128)(2,1)}, u32[]{:S(2)}, u32[]{:S(2)}) collective-permute-start(bf16[64,1,1536]{0,2,1:T(8,128)(2,1)} %collective-permute-done.7), channel_id=1, source_target_pairs={{0,32},{32,64},{64,96},{96,128},{128,160},{160,192},{192,224},{224... | collective-permute-start | bytes 589832 | tf_op jit(solution)/shard_map/ppermute | solution.py:82
  116.4 39.6 %all-to-all-start = ((bf16[32,1,16]{2,1,0:T(2,128)(2,1)}), bf16[32,1,16]{2,1,0:T(2,128)(2,1)S(1)}, u32[]{:S(2)}, u32[]{:S(2)}) async-start(bf16[32,1,16]{2,1,0:T(2,128)(2,1)} %reshape.246), calls=%async_computation | async-start | bytes 32768 | tf_op jit(solution)/shard_map/all_to_all | solution.py:74
  124.1 14.8 %collective-permute-start.9 = (bf16[64,1,1536]{0,2,1:T(8,128)(2,1)}, bf16[64,1,1536]{0,2,1:T(8,128)(2,1)S(1)}, u32[]{:S(2)}, u32[]{:S(2)}) collective-permute-start(bf16[64,1,1536]{0,2,1:T(8,128)(2,1)} %collective-permute-done.8), channel_id=1, source_target_pairs={{0,32},{32,64},{64,96},{96,128},{128,160},{160,192},{192,224},{224... | collective-permute-start | bytes 589832 | tf_op jit(solution)/shard_map/ppermute | solution.py:82
  138.8 13.9 %collective-permute-start.10 = (bf16[64,1,1536]{0,2,1:T(8,128)(2,1)S(1)}, bf16[64,1,1536]{0,2,1:T(8,128)(2,1)}, u32[]{:S(2)}, u32[]{:S(2)}) collective-permute-start(bf16[64,1,1536]{0,2,1:T(8,128)(2,1)S(1)} %collective-permute-done.9), channel_id=1, source_target_pairs={{0,32},{32,64},{64,96},{96,128},{128,160},{160,192},{192,224},{224... | collective-permute-start | bytes 589832 | tf_op jit(solution)/shard_map/ppermute | solution.py:82
  152.7 13.2 %collective-permute-start.11 = (bf16[64,1,1536]{0,2,1:T(8,128)(2,1)}, bf16[64,1,1536]{0,2,1:T(8,128)(2,1)}, u32[]{:S(2)}, u32[]{:S(2)}) collective-permute-start(bf16[64,1,1536]{0,2,1:T(8,128)(2,1)} %collective-permute-done.10), channel_id=1, source_target_pairs={{0,32},{32,64},{64,96},{96,128},{128,160},{160,192},{192,224},{224... | collective-permute-start | bytes 589832 | tf_op jit(solution)/shard_map/ppermute | solution.py:82
  156.1 62.9 %all-to-all-start.2 = ((bf16[32,1,16,1024]{3,2,1,0:T(8,128)(2,1)}), bf16[32,1,16,1024]{3,2,1,0:T(8,128)(2,1)}, u32[]{:S(2)}, u32[]{:S(2)}) async-start(bf16[32,1,16,1024]{3,2,1,0:T(8,128)(2,1)} %bitcast.19), calls=%async_computation.2 | async-start | bytes 2097152 | tf_op jit(solution)/shard_map/all_to_all | solution.py:72
  165.9 13.1 %collective-permute-start.12 = (bf16[64,1,1536]{0,2,1:T(8,128)(2,1)}, bf16[64,1,1536]{0,2,1:T(8,128)(2,1)}, u32[]{:S(2)}, u32[]{:S(2)}) collective-permute-start(bf16[64,1,1536]{0,2,1:T(8,128)(2,1)} %collective-permute-done.11), channel_id=1, source_target_pairs={{0,32},{32,64},{64,96},{96,128},{128,160},{160,192},{192,224},{224... | collective-permute-start | bytes 589832 | tf_op jit(solution)/shard_map/ppermute | solution.py:82
  179.0 12.5 %collective-permute-start.13 = (bf16[64,1,1536]{0,2,1:T(8,128)(2,1)}, bf16[64,1,1536]{0,2,1:T(8,128)(2,1)}, u32[]{:S(2)}, u32[]{:S(2)}) collective-permute-start(bf16[64,1,1536]{0,2,1:T(8,128)(2,1)} %collective-permute-done.12), channel_id=1, source_target_pairs={{0,32},{32,64},{64,96},{96,128},{128,160},{160,192},{192,224},{224... | collective-permute-start | bytes 589832 | tf_op jit(solution)/shard_map/ppermute | solution.py:82
  191.5 11.6 %collective-permute-start.14 = (bf16[64,1,1536]{0,2,1:T(8,128)(2,1)}, bf16[64,1,1536]{0,2,1:T(8,128)(2,1)}, u32[]{:S(2)}, u32[]{:S(2)}) collective-permute-start(bf16[64,1,1536]{0,2,1:T(8,128)(2,1)} %collective-permute-done.13), channel_id=1, source_target_pairs={{0,32},{32,64},{64,96},{96,128},{128,160},{160,192},{192,224},{224... | collective-permute-start | bytes 589832 | tf_op jit(solution)/shard_map/ppermute | solution.py:82
  219.0 23.9 %all-to-all-start.1 = ((bf16[32,1,16,1024]{3,2,1,0:T(8,128)(2,1)}), bf16[32,1,16,1024]{3,2,1,0:T(8,128)(2,1)S(1)}, u32[]{:S(2)}, u32[]{:S(2)}) async-start(bf16[32,1,16,1024]{3,2,1,0:T(8,128)(2,1)} %bitcast.13), calls=%async_computation.1 | async-start | bytes 2097152 | tf_op jit(solution)/shard_map/all_to_all | solution.py:73
  226.8 102.5 %reduce-scatter.4.cloned.1.call-start = ((), (), s32[]{:S(2)}) async-start(), calls=%async_computation.7 | async-start | bytes 3342336
  262.0 22.0 %all-to-all-start.4 = ((bf16[32,1,16,1024]{3,2,1,0:T(8,128)(2,1)}), bf16[32,1,16,1024]{3,2,1,0:T(8,128)(2,1)}, u32[]{:S(2)}, u32[]{:S(2)}) async-start(bf16[32,1,16,1024]{3,2,1,0:T(8,128)(2,1)} %copy.96), calls=%async_computation.4 | async-start | bytes 2097152 | tf_op jit(solution)/shard_map/all_to_all | solution.py:107
  267.8 204.0 %all-reduce.2.cloned.1.call-start = ((), (), s32[]{:S(2)}) async-start(), calls=%async_computation.6 | async-start | bytes 3145728 | tf_op jit(solution)/shard_map/psum | solution.py:123
  284.0 21.3 %all-to-all-start.3 = ((bf16[32,1,16,1024]{3,2,1,0:T(8,128)(2,1)}), bf16[32,1,16,1024]{3,2,1,0:T(8,128)(2,1)S(1)}, u32[]{:S(2)}, u32[]{:S(2)}) async-start(bf16[32,1,16,1024]{3,2,1,0:T(8,128)(2,1)} %copy.95), calls=%async_computation.3 | async-start | bytes 2097152 | tf_op jit(solution)/shard_map/all_to_all | solution.py:102
  (16 other events, 96.4 us)
Sparse Core Ops, SparseCore 0:
  257.0 72.2 reduce-scatter.3
  332.2 139.5 all-reduce.1
